TPU v7x, 512 devices: a whole 4x4x16 slice. The times are simulated.
512 devices in a mesh: seq: 16 (over x, y_hi, core), expert: 32 (over z, y_lo).
Axes of the slice: x: 4, y: 4 (y_hi: 2, y_lo: 2; y = y_hi * 2 + y_lo), z: 16, core: 2. Of those that a mesh axis runs over, the one named last changes fastest.
Arguments:
- tokens: bfloat16 [8192, 1024], P('seq', 'expert'), may hold values from -128 to 128
- mix: bfloat16 [1024, 4096], P(None, 'expert'), may hold values from -2 to 2
- w_in: bfloat16 [64, 1024, 4096], P('expert', None, 'seq'), may hold values from -0.5 to 0.5
- w_out: bfloat16 [64, 4096, 1024], P('expert', 'seq'), may hold values from -0.25 to 0.25
- cotangent: bfloat16 [8192, 1024], P('seq', 'expert'), may hold values from -6 to 6
Outputs:
- mixed: bfloat16 [8192, 1024], P('seq', 'expert')
- grad_tokens: bfloat16 [8192, 1024], P('seq', 'expert')
- grad_mix: bfloat16 [1024, 4096], P(None, 'expert')
- grad_w_in: bfloat16 [64, 1024, 4096], P('expert', None, 'seq')
- grad_w_out: bfloat16 [64, 4096, 1024], P('expert', 'seq')
All inputs are finite; a program needn't handle non-finite values.
Results may differ from a plain program's by a relative error of at most 0.027.
Values may be sent and summed in bfloat16 or wider, within the bound.
A program may use at most 64 MiB of HBM per device.

v0:
```python
import jax
import jax.numpy as jnp
from jax import lax
from jax.sharding import PartitionSpec as P


def inner_rows(left, right):
    return lax.dot_general(
        left, right, (((0,), (0,)), ((), ())), preferred_element_type=jnp.float32
    )


def inner_cols(left, right):
    return lax.dot_general(
        left, right, (((1,), (1,)), ((), ())), preferred_element_type=jnp.float32
    )


def seq_total(partial_value):
    result = lax.psum(partial_value, "seq").astype(jnp.bfloat16)
    return result


def per_device(tokens, mix, w_in, w_out, cotangent):
    whole = lax.all_gather(tokens, "expert", axis=1, tiled=True)
    experts_here, width, hidden_here = w_in.shape
    slot_count = mix.shape[1]
    per_expert = slot_count // experts_here
    logits = jnp.dot(whole, mix, preferred_element_type=jnp.float32)
    col_peak = jnp.max(logits, axis=0)
    col_peak = lax.pmax(col_peak, "seq")
    col_scaled = jnp.exp(logits - col_peak[None, :])
    col_total = lax.psum(jnp.sum(col_scaled, axis=0), "seq")
    dispatch = col_scaled / col_total[None, :]
    dispatch_b = dispatch.astype(jnp.bfloat16)
    slot_in = seq_total(inner_rows(dispatch_b, whole))
    grouped_in = slot_in.reshape(experts_here, per_expert, width)
    pre = jnp.einsum("esd,edh->esh", grouped_in, w_in, preferred_element_type=jnp.float32)
    act = jax.nn.gelu(pre).astype(jnp.bfloat16)
    expert_part = jnp.einsum("esh,ehd->esd", act, w_out, preferred_element_type=jnp.float32)
    slot_out = seq_total(expert_part.reshape(slot_count, width))
    row_peak = jnp.max(logits, axis=1)
    row_peak = lax.pmax(row_peak, "expert")
    row_scaled = jnp.exp(logits - row_peak[:, None])
    row_total = lax.psum(jnp.sum(row_scaled, axis=1), "expert")
    combine = row_scaled / row_total[:, None]
    combine_b = combine.astype(jnp.bfloat16)
    mixed_term = jnp.dot(combine_b, slot_out, preferred_element_type=jnp.float32)
    mixed = lax.psum_scatter(
        mixed_term.astype(jnp.bfloat16), "expert", scatter_dimension=1, tiled=True
    )
    grad_rows = lax.all_gather(cotangent, "expert", axis=1, tiled=True)
    d_comb = inner_cols(grad_rows, slot_out)
    row_sum = lax.psum(jnp.sum(combine * d_comb, axis=1), "expert")
    d_logit_comb = combine * (d_comb - row_sum[:, None])
    d_slot_out = seq_total(inner_rows(combine_b, grad_rows))
    d_grouped = d_slot_out.reshape(experts_here, per_expert, width)
    grad_w_out = jnp.einsum(
        "esh,esd->ehd", act, d_grouped, preferred_element_type=jnp.float32
    ).astype(jnp.bfloat16)
    d_act = jnp.einsum("esd,ehd->esh", d_grouped, w_out, preferred_element_type=jnp.float32)
    _, pull = jax.vjp(jax.nn.gelu, pre)
    d_pre = pull(d_act)[0].astype(jnp.bfloat16)
    grad_w_in = jnp.einsum(
        "esd,esh->edh", grouped_in, d_pre, preferred_element_type=jnp.float32
    ).astype(jnp.bfloat16)
    back_part = jnp.einsum("esh,edh->esd", d_pre, w_in, preferred_element_type=jnp.float32)
    d_slot_in = seq_total(back_part.reshape(slot_count, width))
    d_disp = inner_cols(whole, d_slot_in)
    col_sum = lax.psum(jnp.sum(dispatch * d_disp, axis=0), "seq")
    d_logit = (dispatch * (d_disp - col_sum[None, :]) + d_logit_comb).astype(jnp.bfloat16)
    grad_mix = lax.psum(inner_rows(whole, d_logit).astype(jnp.bfloat16), "seq")
    token_term = jnp.dot(dispatch_b, d_slot_in, preferred_element_type=jnp.float32) + inner_cols(
        d_logit, mix
    )
    grad_tokens = lax.psum_scatter(
        token_term.astype(jnp.bfloat16), "expert", scatter_dimension=1, tiled=True
    )
    return (mixed, grad_tokens, grad_mix, grad_w_in, grad_w_out)


def solution(mesh):
    placed = (
        P("seq", "expert"),
        P(None, "expert"),
        P("expert", None, "seq"),
        P("expert", "seq", None),
        P("seq", "expert"),
    )
    return jax.shard_map(
        per_device,
        mesh=mesh,
        in_specs=placed,
        out_specs=(
            P("seq", "expert"),
            P("seq", "expert"),
            P(None, "expert"),
            P("expert", None, "seq"),
            P("expert", "seq", None),
        ),
        check_vma=False,
    )
```

profile of v0, /device:TPU:6, one launch (start us, length us, event | category | flops | bytes accessed | tf_op | source)
XLA Modules:
  0.0 1030.0 jit_solution(13742207474744335898)
XLA Ops:
  8.7 137.2 %all-gather.3.cloned.1.call-done = bf16[512,1024]{0,1:T(8,128)(2,1)} async-done(((bf16[512,32]{0,1:T(8,128)(2,1)}), bf16[512,1024]{0,1:T(8,128)(2,1)}) %all-gather.3.cloned.1.call-update) | async-done | bytes 1048592 | tf_op jit(solution)/shard_map/all_gather | solution.py:25
  145.9 1.8 fusion.28
  147.7 28.4 %pmax.15 = f32[128]{0:T(128)S(1)} all-reduce(f32[128]{0:T(128)S(1)} %get-tuple-element.15), channel_id=1, replica_groups=mesh['seq'=16,'expert'=32] {'seq'}, use_global_device_ids=true, to_apply=%region_5.0 | all-reduce | flops 128 | bytes 1024 | tf_op jit(solution)/shard_map/pmax | solution.py:31
  176.1 62.4 %pmax.14 = f32[512]{0:T(512)S(1)} all-reduce(f32[512]{0:T(512)S(1)} %get-tuple-element.14), channel_id=1, replica_groups=mesh['seq'=16,'expert'=32] {'expert'}, use_global_device_ids=true, to_apply=%region_1.0 | all-reduce | flops 512 | bytes 4096 | tf_op jit(solution)/shard_map/pmax | solution.py:43
  238.8 29.2 %psum.64 = f32[128]{0:T(128)S(1)} all-reduce(f32[128]{0:T(128)S(1)} %get-tuple-element.13), channel_id=1, replica_groups=mesh['seq'=16,'expert'=32] {'seq'}, use_global_device_ids=true, to_apply=%region_7.0 | all-reduce | flops 128 | bytes 1024 | tf_op jit(solution)/shard_map/psum | solution.py:33
  268.0 1.8 fusion.18
  269.8 60.1 %psum.63 = f32[512]{0:T(512)S(1)} all-reduce(f32[512]{0:T(512)S(1)} %get-tuple-element.12), channel_id=1, replica_groups=mesh['seq'=16,'expert'=32] {'expert'}, use_global_device_ids=true, to_apply=%region_3.0 | all-reduce | flops 512 | bytes 4096 | tf_op jit(solution)/shard_map/psum | solution.py:45
  329.9 2.7 fusion.20
  332.6 76.4 %all-reduce.7 = (bf16[128,1024]{1,0:T(8,128)(2,1)S(1)}, bf16[128,1024]{1,0:T(8,128)(2,1)S(1)}) all-reduce(f32[128,1024]{1,0:T(8,128)S(1)} %fusion.18, f32[128,1024]{1,0:T(8,128)} %fusion.20), channel_id=1, replica_groups=mesh['seq'=16,'expert'=32] {'seq'}, use_global_device_ids=true, to_apply=%region_8.0 | all-reduce | flops 262144 | bytes 1572864 | tf_op jit(solution)/shard_map/psum | solution.py:20
  409.9 1.2 fusion.30
  412.3 77.2 %all-reduce.8 = (bf16[128,1024]{1,0:T(8,128)(2,1)S(1)}, bf16[128,1024]{1,0:T(8,128)(2,1)S(1)}) all-reduce(f32[128,1024]{1,0:T(8,128)} %bitcast.35, f32[128,1024]{1,0:T(8,128)} %bitcast.34), channel_id=1, replica_groups=mesh['seq'=16,'expert'=32] {'seq'}, use_global_device_ids=true, to_apply=%region_9.0 | all-reduce | flops 262144 | bytes 1572864 | tf_op jit(solution)/shard_map/psum | solution.py:20
  489.4 1.8 convolution_bitcast_fusion
  491.2 1.3 multiply_reduce_fusion.1
  492.6 33.6 %psum.69 = f32[128]{0:T(128)S(1)} all-reduce(f32[128]{0:T(128)S(1)} %get-tuple-element.10), channel_id=1, replica_groups=mesh['seq'=16,'expert'=32] {'seq'}, use_global_device_ids=true, to_apply=%region_14.0 | all-reduce | flops 128 | bytes 1024 | tf_op jit(solution)/shard_map/psum | solution.py:70
  526.2 62.3 %psum.70 = f32[512]{0:T(512)S(1)} all-reduce(f32[512]{0:T(512)S(1)} %get-tuple-element.11), channel_id=1, replica_groups=mesh['seq'=16,'expert'=32] {'expert'}, use_global_device_ids=true, to_apply=%region_16.0 | all-reduce | flops 512 | bytes 4096 | tf_op jit(solution)/shard_map/psum | solution.py:54
  588.5 1.2 add_convert_fusion.1
  591.0 1.6 convolution_convert_fusion
  593.5 1.5 add_convert_fusion
  595.1 1.5 convolution_convert_fusion.2
  596.5 1.5 convolution_convert_fusion.1
  598.0 141.2 %all-reduce.6.cloned.1.call-done = bf16[1024,128]{0,1:T(8,128)(2,1)} async-done(((bf16[1024,128]{0,1:T(8,128)(2,1)}), bf16[1024,128]{0,1:T(8,128)(2,1)}) %all-reduce.6.cloned.1.call-update) | async-done | bytes 262160 | tf_op jit(solution)/shard_map/psum | solution.py:72
  739.2 1.8 copy.12
  741.0 145.1 %reduce-scatter.3.cloned.1.call-done = bf16[512,32]{0,1:T(8,128)(2,1)} async-done(((bf16[512,1024]{0,1:T(8,128)(2,1)}), bf16[512,32]{0,1:T(8,128)(2,1)}) %reduce-scatter.3.cloned.1.call-update) | async-done | bytes 32784 | tf_op jit(solution)/shard_map/reduce_scatter | solution.py:49
  886.1 137.3 %reduce-scatter.5.cloned.1.call-done = bf16[512,32]{0,1:T(8,128)(2,1)} async-done(((bf16[512,1024]{0,1:T(8,128)(2,1)}), bf16[512,32]{0,1:T(8,128)(2,1)}) %reduce-scatter.5.cloned.1.call-update) | async-done | bytes 32784 | tf_op jit(solution)/shard_map/reduce_scatter | solution.py:76
  (37 shorter events, 5.9 us)
Async XLA Ops:
  7.2 402.4 %copy-start = (bf16[2,1024,256]{2,1,0:T(8,128)(2,1)S(1)}, bf16[2,1024,256]{2,1,0:T(8,128)(2,1)}, u32[]{:S(2)}) copy-start(bf16[2,1024,256]{2,1,0:T(8,128)(2,1)} %param.7) | copy-start | bytes 3145732
  7.2 138.7 %all-gather.3.cloned.1.call-start = ((), (), s32[]{:S(2)}) async-start(), calls=%async_computation.2 | async-start | bytes 1081344 | tf_op jit(solution)/shard_map/all_gather | solution.py:25
  7.9 322.0 %all-gather.5.cloned.1.call-start = ((), (), s32[]{:S(2)}) async-start(), calls=%async_computation.4 | async-start | bytes 1081344 | tf_op jit(solution)/shard_map/all_gather | solution.py:52
  8.7 730.6 %all-reduce.6.cloned.1.call-start = ((), (), s32[]{:S(2)}) async-start(), calls=%async_computation.6 | async-start | bytes 524288 | tf_op jit(solution)/shard_map/psum | solution.py:72
  268.0 141.1 %copy-start.2 = (bf16[2,256,1024]{2,1,0:T(8,128)(2,1)S(1)}, bf16[2,256,1024]{2,1,0:T(8,128)(2,1)}, u32[]{:S(2)}) copy-start(bf16[2,256,1024]{2,1,0:T(8,128)(2,1)} %param.8) | copy-start | bytes 3145732
  409.1 2.1 copy-start.4
  409.1 2.1 copy-start.6
  409.9 2.3 copy-start.8
  411.2 80.0 %copy-start.1 = (bf16[512,1024]{0,1:T(8,128)(2,1)S(1)}, bf16[512,1024]{0,1:T(8,128)(2,1)}, u32[]{:S(2)}) copy-start(bf16[512,1024]{0,1:T(8,128)(2,1)} %all-gather.3.cloned.1.call-done) | copy-start | bytes 3145732
  590.9 295.2 %reduce-scatter.3.cloned.1.call-start = ((), (), s32[]{:S(2)}) async-start(), calls=%async_computation.3 | async-start | bytes 1081344 | tf_op jit(solution)/shard_map/reduce_scatter | solution.py:49
  592.6 0.9 copy-start.3
  592.6 430.8 %reduce-scatter.5.cloned.1.call-start = ((), (), s32[]{:S(2)}) async-start(), calls=%async_computation.5 | async-start | bytes 1081344 | tf_op jit(solution)/shard_map/reduce_scatter | solution.py:76
  593.5 1.5 copy-start.5
  593.5 1.5 copy-start.9
  595.0 1.5 copy-start.7
Sparse Core Ops, SparseCore 0:
  10.1 135.7 all-gather.2
  148.0 129.8 all-gather.4
  591.0 148.1 all-reduce.5
  742.7 143.3 reduce-scatter.2
  889.3 134.0 reduce-scatter.4
where the time goes:
time: 1030 us
  waiting for transfers between devices  562 us (55%)
  blocking collectives  430 us (42%)
  matrix products  20.2 us (2%)
  between operations  13.9 us (1%)
    psum x2, blocking collectives, seq_total(): result = lax.psum(partial_value, 'seq').astype(jnp.bfloat16)  154 us
    reduce_scatter x1, waiting for transfers between devices, per_device(): lax.psum_scatter(mixed_term.astype(jnp.bfloat16), 'expert', scatter_dimen...  145 us
    psum x1, waiting for transfers between devices, per_device(): grad_mix = lax.psum(inner_rows(whole, d_logit).astype(jnp.bfloat16), 'seq')  141 us
    reduce_scatter x1, waiting for transfers between devices, per_device(): lax.psum_scatter(token_term.astype(jnp.bfloat16), 'expert', scatter_dimen...  137 us
    all_gather x1, waiting for transfers between devices, per_device(): whole = lax.all_gather(tokens, 'expert', axis=1, tiled=True)  137 us
    pmax x1, blocking collectives, per_device(): row_peak = lax.pmax(row_peak, 'expert')  62.4 us
    psum x1, blocking collectives, per_device(): row_sum = lax.psum(jnp.sum(combine * d_comb, axis=1), 'expert')  62.3 us
    psum x1, blocking collectives, per_device(): row_total = lax.psum(jnp.sum(row_scaled, axis=1), 'expert')  60.1 us
  transfers between devices with their start and end apart: 5, of which 4 were waited for; matrix products, arithmetic and copies ran while one was open for 1% of the time, Pallas kernels for 0%

commit v1 on v0

v1 whole, which is shorter than its diff:
```python
import functools
import math

import jax
import jax.numpy as jnp
from jax import lax
from jax.experimental import pallas as pl
from jax.experimental.pallas import tpu as pltpu
from jax.sharding import PartitionSpec as P

MESH = pl.DeviceIdType.MESH
F32 = jnp.float32
BF = jnp.bfloat16
GELU_K = math.sqrt(2.0 / math.pi)

D = 1024
TOK = 256
SLOT = 256
OWN = 128
HID = 256
HALF = 512

(Z_TOK1, Z_TOK2, Z_COT1, Z_COT2, ROWST, COLST, ROWSUM, COLSUM, MIXX,
 X_SI, R_SI, A_SI, F_SI, X_DO, R_DO, A_DO, F_DO, X_SO, R_SO, A_SO, F_SO,
 X_DI, R_DI, A_DI, F_DI, X_GM, R_GM, A_GM, F_GM,
 ZM1, ZM2, ZG1, ZG2, NSEM) = range(34)
(L_TOK, L_COT, L_MIX, L_WI, L_WO, L_GWI, L_GWO, L_MX, L_GT, L_GM, NLOC) = range(11)


def dot(a, b):
    return jnp.dot(a, b, preferred_element_type=F32)


def kernel(tok_h, mix_h, win_h, wout_h, cot_h,
           mixed_o, gtok_o, gmix_o, gwin_o, gwout_o,
           tokv, cotv, tt, ct, tn, cn, mh, mt, wi, wo, wit, wot,
           rowst, colst, rowb, colb, rsum, csum, rsumb, csumb,
           pb, xb, sb, rb, ab, pb2, xb2, sb2, rb2, ab2,
           pz, rz, sz, fz, lt, disp, dispb, combt, combb, dcomb, ddisp, dlog, part1,
           prev, actv, dprev, gwi, gwo, outv, gmv, seven,
           ss, rs, ls):
    s = lax.axis_index("seq")
    e = lax.axis_index("expert")
    u, c = s // 2, s % 2
    z, yl = e // 2, e % 2
    zh, zl = z // 4, z % 4
    r = yl * 8 + u
    p = r * 2 + c

    def dev(u_, yl_, z_, c_):
        return (u_ * 2 + c_, z_ * 2 + yl_)

    def chip(r_, c_):
        return dev(r_ % 8, r_ // 8, z, c_)

    def send(src, dst, k, to, rk=None):
        pltpu.make_async_remote_copy(
            src_ref=src, dst_ref=dst, send_sem=ss.at[k], recv_sem=rs.at[k if rk is None else rk],
            device_id=to, device_id_type=MESH).start()

    def wait(ref, sem):
        pltpu.make_async_copy(ref, ref, sem).wait()

    def wait_recv(ref, k):
        wait(ref, rs.at[k])

    def wait_send(ref, k):
        wait(ref, ss.at[k])

    def local(src, dst, k):
        cp = pltpu.make_async_copy(src, dst, ls.at[k])
        cp.start()
        return cp

    def each(n, f):
        def body(i, carry):
            f(i)
            return carry
        lax.fori_loop(0, n, body, 0)

    for h in range(2):
        local(tok_h.at[:, pl.ds(h * TOK, TOK)], tokv.at[h], L_TOK)
    for h in range(2):
        local(cot_h.at[:, pl.ds(h * TOK, TOK)], cotv.at[h], L_COT)
    local(mix_h, mh.at[yl], L_MIX)
    local(win_h, wi, L_WI)
    local(wout_h, wo, L_WO)

    bar = pltpu.get_barrier_semaphore()

    def sig(to):
        pl.semaphore_signal(bar, inc=1, device_id=to, device_id_type=MESH)

    def sig_plane(i):
        q = (p + 1 + i) % 32
        sig(chip(q // 2, q % 2))
    each(31, sig_plane)
    each(15, lambda i: sig(dev(u, yl, (z + 1 + i) % 16, c)))
    each(3, lambda i: sig(dev(u, 1 - yl, (z + 4 * (i + 1)) % 16, c)))
    pl.semaphore_wait(bar, 49)

    def gather1(src, dst, k):
        def one(i):
            zz = (z + 4 * (i // 2)) % 16
            yy = (yl + i % 2) % 2
            send(src.at[yy], dst.at[zh, zl, yl], k, dev(u, yy, zz, c))

        def step(i):
            one(i + 1)
        each(7, step)
        dst[zh, zl, yl] = src[yl]

    def gather2(buf, k1, k2):
        wait_recv(seven, k1)
        send(buf.at[:, zl], buf.at[:, zl], k2, dev(u, yl, (z + 1) % 16, c))
        send(buf.at[:, zl], buf.at[:, zl], k2, dev(u, yl, (z + 15) % 16, c))
        send(buf.at[pl.ds(0, 2), zl], buf.at[pl.ds(0, 2), zl], k2, dev(u, yl, (z + 2) % 16, c))
        send(buf.at[pl.ds(2, 2), zl], buf.at[pl.ds(2, 2), zl], k2, dev(u, yl, (z + 14) % 16, c))

    wait(tokv, ls.at[L_TOK])
    gather1(tokv, tt, Z_TOK1)
    wait(mh.at[0], ls.at[L_MIX])
    send(mh.at[yl], mh.at[yl], MIXX, dev(u, 1 - yl, z, c))
    mt[pl.ds(pl.multiple_of(yl * OWN, OWN), OWN), :] = mh[yl].T
    wait(cotv, ls.at[L_COT])
    gather2(tt, Z_TOK1, Z_TOK2)
    gather1(cotv, ct, Z_COT1)
    wait_recv(mh.at[0], MIXX)
    mt[pl.ds(pl.multiple_of((1 - yl) * OWN, OWN), OWN), :] = mh[1 - yl].T
    wait(wi, ls.at[L_WI])
    wait(wo, ls.at[L_WO])
    for k in range(2):
        wit[k] = wi[k].T
        wot[k] = wo[k].T
    wait_recv(tt.at[:, pl.ds(0, 3)], Z_TOK2)

    ttv = tt[...].reshape(D, TOK)
    logits = dot(mt[...], ttv)
    lt[...] = logits
    rm = jnp.max(logits, axis=0, keepdims=True)
    rsm = jnp.sum(jnp.exp(logits - rm), axis=0, keepdims=True)

    def put(ref, at, v):
        ref[at:at + 1, :] = v[:, :128]
        ref[at + 1:at + 2, :] = v[:, 128:]

    put(rowst, 0, rm)
    put(rowst, 2, rsm)

    def z_all(src, dst, k):
        def one(i):
            d = (8 + i // 2 + 1) - 2 * ((i // 2 + 1) * (i % 2))
            send(src, dst.at[z], k, dev(u, yl, (z + d) % 16, c))
        send(src, dst.at[z], k, dev(u, yl, (z + 8) % 16, c))
        each(14, one)
        dst[z] = src[...]

    def plane_all(src, dst, k):
        def one(i):
            q = (p + 1 + i) % 32
            send(src, dst.at[p], k, chip(q // 2, q % 2))
        each(31, one)
        dst[p] = src[...]

    def to_row(col):
        return jnp.broadcast_to(col, (SLOT, 128)).T[0:1, :]

    def to_cols(two):
        row = jnp.concatenate([two[0:1, :], two[1:2, :]], axis=1)
        half = jnp.broadcast_to(row, (128, SLOT)).T
        return jnp.concatenate([half, half], axis=1)

    z_all(rowst, rowb, ROWST)
    cm = jnp.max(logits, axis=1, keepdims=True)
    csm = jnp.sum(jnp.exp(logits - cm), axis=1, keepdims=True)
    put(colst, 0, to_row(cm))
    put(colst, 2, to_row(csm))
    plane_all(colst, colb, COLST)

    gather2(ct, Z_COT1, Z_COT2)
    tn[...] = ttv.T

    def totals(buf):
        v = buf[...]
        m = v[:, 0:2, :]
        top = jnp.max(m, axis=0)
        total = jnp.sum(v[:, 2:4, :] * jnp.exp(m - top[None]), axis=0)
        return top, total

    def core_swap(buf, xbuf, k):
        send(buf.at[1 - c], xbuf, k, dev(u, yl, z, 1 - c))

    def store_halves(buf, v):
        n = v.shape[0]
        for h in range(2):
            buf[h] = v[:, h * HALF:(h + 1) * HALF].astype(BF).reshape(n // 16, 16, HALF)

    wait_recv(colb.at[pl.ds(0, 31)], COLST)
    top, total = totals(colb)
    dv = jnp.exp(lt[...] - to_cols(top)) / to_cols(total)
    disp[...] = dv
    dispb[...] = dv.astype(BF)
    store_halves(pb.at[0], dot(dispb[...], tn[...]))
    core_swap(pb.at[0], xb.at[0], X_SI)

    wait_recv(rowb.at[pl.ds(0, 15)], ROWST)
    top, total = totals(rowb)
    topr = jnp.concatenate([top[0:1, :], top[1:2, :]], axis=1)
    totr = jnp.concatenate([total[0:1, :], total[1:2, :]], axis=1)
    cv = jnp.exp(lt[...] - topr) / totr
    combt[...] = cv
    combb[...] = cv.astype(BF)

    def rs32_send(j, kx, kr):
        wait_recv(xb.at[j], kx)
        sb[j] = (pb[j, c].astype(F32) + xb[j].astype(F32)).astype(BF)

        def one(i):
            q = (r + 1 + i) % 16
            send(sb.at[j, q], rb.at[j, r], kr, chip(q, c))
        each(15, one)
        rb[j, r] = sb[j, r]

    def rs32_sum(j, kr):
        wait_recv(rb.at[j, pl.ds(0, 15)], kr)
        return jnp.sum(rb[j].astype(F32), axis=0).astype(BF)

    def ag16_send(j, v, ka):
        ab[j, c, u] = v

        def one(i):
            q = (u + 1 + i) % 8
            send(ab.at[j, c, u], ab.at[j, c, u], ka, dev(q, yl, z, c))
        each(7, one)

    def ag16_forward(j, ka, kf):
        wait_recv(ab.at[j, 0, pl.ds(0, 7)], ka)
        send(ab.at[j, c], ab.at[j, c], kf, dev(u, yl, z, 1 - c))

    rs32_send(0, X_SI, R_SI)
    wait_recv(ct.at[:, pl.ds(0, 3)], Z_COT2)
    cn[...] = ct[...].reshape(D, TOK).T
    store_halves(pb.at[1], dot(combb[...], cn[...]))
    core_swap(pb.at[1], xb.at[1], X_DO)
    rs32_send(1, X_DO, R_DO)
    ag16_send(0, rs32_sum(0, R_SI), A_SI)
    ag16_forward(0, A_SI, F_SI)
    ag16_send(1, rs32_sum(1, R_DO), A_DO)

    def halves(j):
        return [ab[j, h].reshape(OWN, HALF) for h in range(2)]

    def rs16_send(j, kx, kr):
        wait_recv(xb2.at[j], kx)
        sb2[j] = (pb2[j, c].astype(F32) + xb2[j].astype(F32)).astype(BF)

        def one(i):
            q = (u + 1 + i) % 8
            send(sb2.at[j, q], rb2.at[j, u], kr, dev(q, yl, z, c))
        each(7, one)
        rb2[j, u] = sb2[j, u]

    def rs16_sum(j, kr):
        wait_recv(rb2.at[j, pl.ds(0, 7)], kr)
        return jnp.sum(rb2[j].astype(F32), axis=0).astype(BF)

    def ag32_send(j, v, ka):
        ab2[j, c, r] = v

        def one(i):
            q = (r + 1 + i) % 16
            send(ab2.at[j, c, r], ab2.at[j, c, r], ka, chip(q, c))
        each(15, one)

    def ag32_forward(j, ka, kf):
        wait_recv(ab2.at[j, 0, pl.ds(0, 15)], ka)
        send(ab2.at[j, c], ab2.at[j, c], kf, dev(u, yl, z, 1 - c))

    def rows(k):
        return slice(k * 64, (k + 1) * 64)

    wait_recv(ab.at[0, 0], F_SI)
    x0, x1 = halves(0)
    outs = []
    for k in range(2):
        pre = dot(x0[rows(k)], wi[k, :HALF, :]) + dot(x1[rows(k)], wi[k, HALF:, :])
        prev[k] = pre
        t = jnp.tanh(GELU_K * (pre + 0.044715 * (pre * pre * pre)))
        act = (0.5 * pre * (1.0 + t)).astype(BF)
        actv[k] = act
        outs.append(dot(act, wo[k]))
    store_halves(pb2.at[0], jnp.concatenate(outs, axis=0))
    core_swap(pb2.at[0], xb2.at[0], X_SO)

    ag16_forward(1, A_DO, F_DO)
    rs16_send(0, X_SO, R_SO)
    wait_recv(ab.at[1, 0], F_DO)
    g0, g1 = halves(1)
    outs = []
    for k in range(2):
        dact = dot(g0[rows(k)], wot[k, :HALF, :]) + dot(g1[rows(k)], wot[k, HALF:, :])
        pre = prev[k]
        sq = pre * pre
        t = jnp.tanh(GELU_K * (pre + 0.044715 * (sq * pre)))
        slope = 0.5 * (1.0 + t) + 0.5 * pre * (1.0 - t * t) * (GELU_K * (1.0 + 3.0 * 0.044715 * sq))
        dpre = (dact * slope).astype(BF)
        dprev[k] = dpre
        outs.append(dot(dpre, wit[k]))
    store_halves(pb2.at[1], jnp.concatenate(outs, axis=0))
    core_swap(pb2.at[1], xb2.at[1], X_DI)
    rs16_send(1, X_DI, R_DI)
    ag32_send(0, rs16_sum(0, R_SO), A_SO)

    for k in range(2):
        xt0, xt1 = x0[rows(k)].T, x1[rows(k)].T
        gwi[k, :HALF, :] = dot(xt0, dprev[k]).astype(BF)
        gwi[k, HALF:, :] = dot(xt1, dprev[k]).astype(BF)
        at = actv[k].T
        gwo[k, :, :HALF] = dot(at, g0[rows(k)]).astype(BF)
        gwo[k, :, HALF:] = dot(at, g1[rows(k)]).astype(BF)
    local(gwi, gwin_o, L_GWI)
    local(gwo, gwout_o, L_GWO)

    ag32_send(1, rs16_sum(1, R_DI), A_DI)
    ag32_forward(0, A_SO, F_SO)
    ag32_forward(1, A_DI, F_DI)

    def full(j):
        return [ab2[j, h].reshape(SLOT, HALF) for h in range(2)]

    def scatter1(j, k):
        def to(step):
            return dev(u, yl, (z + step) % 16, c)
        send(pz.at[j, :, (zl + 1) % 4], rz.at[j, 0], k, to(1))
        send(pz.at[j, :, (zl + 3) % 4], rz.at[j, 1], k, to(15))
        send(pz.at[j, pl.ds(0, 2), (zl + 2) % 4], rz.at[j, 2, pl.ds(0, 2)], k, to(2))
        send(pz.at[j, pl.ds(2, 2), (zl + 2) % 4], rz.at[j, 2, pl.ds(2, 2)], k, to(14))

    def scatter2(j, k1, k2):
        wait_recv(rz.at[j], k1)
        v = pz[j, :, zl].astype(F32)
        for i in range(3):
            v = v + rz[j, i].astype(F32)
        sz[j] = v.astype(BF)

        def one(i):
            zz = (zh + (i + 1) // 2) % 4
            yy = (yl + (i + 1) % 2) % 2
            send(sz.at[j, zz, yy], fz.at[j, zh, yl], k2, dev(u, yy, zz * 4 + zl, c))
        each(7, one)
        fz[j, zh, yl] = sz[j, zh, yl]

    def scatter3(j, k2, out, lk):
        wait_recv(seven, k2)
        v = jnp.sum(fz[j].astype(F32), axis=0).astype(BF)
        for h in range(2):
            outv[j, :, h * TOK:(h + 1) * TOK] = v[h]
        local(outv.at[j], out, lk)

    wait_recv(ab2.at[0, 0], F_SO)
    so0, so1 = full(0)
    ctv = ct[...].reshape(D, TOK)
    dcv = dot(so0, ctv[:HALF]) + dot(so1, ctv[HALF:])
    dcomb[...] = dcv
    put(rsum, 0, jnp.sum(combt[...] * dcv, axis=0, keepdims=True))
    z_all(rsum, rsumb, ROWSUM)

    wait_recv(ab2.at[1, 0], F_DI)
    di0, di1 = full(1)
    ddv = dot(di0, ttv[:HALF]) + dot(di1, ttv[HALF:])
    ddisp[...] = ddv
    put(csum, 0, to_row(jnp.sum(disp[...] * ddv, axis=1, keepdims=True)))
    plane_all(csum, csumb, COLSUM)

    pz[0, 0:2] = dot(so0.T, combb[...]).astype(BF).reshape(2, 4, 2, 32, TOK)
    pz[0, 2:4] = dot(so1.T, combb[...]).astype(BF).reshape(2, 4, 2, 32, TOK)
    scatter1(0, ZM1)
    part1[0:HALF, :] = dot(di0.T, dispb[...])
    part1[HALF:, :] = dot(di1.T, dispb[...])
    wait_recv(csumb.at[pl.ds(0, 31)], COLSUM)
    cols = to_cols(jnp.sum(csumb[...], axis=0))
    wait_recv(rsumb.at[pl.ds(0, 15)], ROWSUM)
    rtot = jnp.sum(rsumb[...], axis=0)
    rowr = jnp.concatenate([rtot[0:1, :], rtot[1:2, :]], axis=1)
    dlv = (disp[...] * (ddisp[...] - cols) + combt[...] * (dcomb[...] - rowr)).astype(BF)
    dlog[...] = dlv
    mfull = jnp.concatenate([mh[0], mh[1]], axis=1)
    pz[1] = (part1[...] + dot(mfull, dlv)).astype(BF).reshape(4, 4, 2, 32, TOK)
    scatter1(1, ZG1)
    store_halves(pb.at[2], dot(dlog[...], tn[...]))
    core_swap(pb.at[2], xb.at[2], X_GM)
    scatter2(0, ZM1, ZM2)
    rs32_send(2, X_GM, R_GM)
    scatter2(1, ZG1, ZG2)
    scatter3(0, ZM2, mixed_o, L_MX)
    ag16_send(2, rs32_sum(2, R_GM), A_GM)
    ag16_forward(2, A_GM, F_GM)
    wait_recv(ab.at[2, 0], F_GM)
    for h in range(2):
        gmv[h * HALF:(h + 1) * HALF, :] = ab[2, h].reshape(OWN, HALF).T
    local(gmv, gmix_o, L_GM)
    scatter3(1, ZG2, gtok_o, L_GT)

    for buf, k1, k2 in ((tt, Z_TOK1, Z_TOK2), (ct, Z_COT1, Z_COT2)):
        wait_send(seven, k1)
        wait_send(buf.at[:, pl.ds(0, 3)], k2)
    wait_send(mh.at[0], MIXX)
    wait_send(rowb.at[pl.ds(0, 15)], ROWST)
    wait_send(colb.at[pl.ds(0, 31)], COLST)
    wait_send(rsumb.at[pl.ds(0, 15)], ROWSUM)
    wait_send(csumb.at[pl.ds(0, 31)], COLSUM)
    for j, kx, kr, ka, kf in ((0, X_SI, R_SI, A_SI, F_SI), (1, X_DO, R_DO, A_DO, F_DO), (2, X_GM, R_GM, A_GM, F_GM)):
        wait_send(xb.at[j], kx)
        wait_send(rb.at[j, pl.ds(0, 15)], kr)
        wait_send(ab.at[j, 0, pl.ds(0, 7)], ka)
        wait_send(ab.at[j, 0], kf)
    for j, kx, kr, ka, kf in ((0, X_SO, R_SO, A_SO, F_SO), (1, X_DI, R_DI, A_DI, F_DI)):
        wait_send(xb2.at[j], kx)
        wait_send(rb2.at[j, pl.ds(0, 7)], kr)
        wait_send(ab2.at[j, 0, pl.ds(0, 15)], ka)
        wait_send(ab2.at[j, 0], kf)
    for j, k1, k2 in ((0, ZM1, ZM2), (1, ZG1, ZG2)):
        wait_send(rz.at[j], k1)
        wait_send(seven, k2)
    wait(gwi, ls.at[L_GWI])
    wait(gwo, ls.at[L_GWO])
    wait(outv.at[0], ls.at[L_MX])
    wait(outv.at[1], ls.at[L_GT])
    wait(gmv, ls.at[L_GM])


def per_device(tokens, mix, w_in, w_out, cotangent):
    scratch = [
        ((2, 32, TOK), BF), ((2, 32, TOK), BF),
        ((4, 4, 2, 32, TOK), BF), ((4, 4, 2, 32, TOK), BF),
        ((TOK, D), BF), ((TOK, D), BF),
        ((2, D, OWN), BF), ((SLOT, D), BF),
        ((2, D, HID), BF), ((2, HID, D), BF),
        ((2, HID, D), BF), ((2, D, HID), BF),
        ((8, 128), F32), ((8, 128), F32), ((16, 8, 128), F32), ((32, 8, 128), F32),
        ((8, 128), F32), ((8, 128), F32), ((16, 8, 128), F32), ((32, 8, 128), F32),
        ((3, 2, 16, 16, HALF), BF), ((3, 16, 16, HALF), BF), ((3, 16, 16, HALF), BF),
        ((3, 16, 16, HALF), BF), ((3, 2, 8, 16, HALF), BF),
        ((2, 2, 8, 16, HALF), BF), ((2, 8, 16, HALF), BF), ((2, 8, 16, HALF), BF),
        ((2, 8, 16, HALF), BF), ((2, 2, 16, 16, HALF), BF),
        ((2, 4, 4, 2, 32, TOK), BF), ((2, 3, 4, 2, 32, TOK), BF),
        ((2, 4, 2, 32, TOK), BF), ((2, 4, 2, 32, TOK), BF),
        ((SLOT, TOK), F32), ((SLOT, TOK), F32), ((SLOT, TOK), BF), ((SLOT, TOK), F32), ((SLOT, TOK), BF),
        ((SLOT, TOK), F32), ((SLOT, TOK), F32), ((SLOT, TOK), BF), ((D, TOK), F32),
        ((2, 64, HID), F32), ((2, 64, HID), BF), ((2, 64, HID), BF),
        ((2, D, HID), BF), ((2, HID, D), BF), ((2, 32, 2 * TOK), BF), ((D, OWN), BF),
        ((7, 32, TOK), BF),
    ]
    hbm = pl.BlockSpec(memory_space=pl.ANY)
    mixed_t, gtok_t, gmix, gwin, gwout = pl.pallas_call(
        kernel,
        out_shape=(
            jax.ShapeDtypeStruct((32, 512), BF),
            jax.ShapeDtypeStruct((32, 512), BF),
            jax.ShapeDtypeStruct(mix.shape, BF),
            jax.ShapeDtypeStruct(w_in.shape, BF),
            jax.ShapeDtypeStruct(w_out.shape, BF),
        ),
        in_specs=[hbm] * 5,
        out_specs=[hbm] * 5,
        scratch_shapes=[pltpu.VMEM(shape, kind) for shape, kind in scratch] + [
            pltpu.SemaphoreType.DMA((NSEM,)),
            pltpu.SemaphoreType.DMA((NSEM,)),
            pltpu.SemaphoreType.DMA((NLOC,)),
        ],
        compiler_params=pltpu.CompilerParams(
            collective_id=0, has_side_effects=True, vmem_limit_bytes=48 * 1024 * 1024
        ),
        name="soft_moe",
    )(tokens.T, mix, w_in, w_out, cotangent.T)
    return mixed_t.T, gtok_t.T, gmix, gwin, gwout


def solution(mesh):
    placed = (
        P("seq", "expert"),
        P(None, "expert"),
        P("expert", None, "seq"),
        P("expert", "seq", None),
        P("seq", "expert"),
    )
    return jax.shard_map(
        per_device,
        mesh=mesh,
        in_specs=placed,
        out_specs=(
            P("seq", "expert"),
            P("seq", "expert"),
            P(None, "expert"),
            P("expert", None, "seq"),
            P("expert", "seq", None),
        ),
        check_vma=False,
    )
```

time: 1030 us -> 128 us (0.12)
  the two profiles are of different devices: /device:TPU:6 before, /device:TPU:1 now
where the time goes in v1:
time: 128 us; the launch traced here: 127 us
  Pallas kernels  118 us (92%)
  local copies, waits for them, and re-layouts  8.78 us (7%)
    pallas_call x1, Pallas kernels, per_device(): pl.pallas_call(kernel, out_shape=(jax.ShapeDtypeStruct((32, 512), BF), ja...  118 us
    unnamed x15, local copies, waits for them, and re-layouts  8.78 us

profile of v1, /device:TPU:1, one launch (start us, length us, event | category | flops | bytes accessed | tf_op | source)
XLA Modules:
  0.0 127.2 jit_solution(5204636464798194723)
XLA Ops:
  0.6 0.0 copy-start
  0.6 1.2 copy-done
  1.9 0.0 copy-start.1
  1.9 1.2 copy-done.1
  3.1 0.0 copy-start.2
  3.1 0.9 copy-done.2
  4.0 0.0 copy-start.3
  4.0 0.8 copy-done.3
  4.8 0.0 copy-start.4
  4.8 0.8 copy-done.4
  5.6 117.8 %soft_moe.1 = (bf16[32,512]{1,0:T(8,128)(2,1)S(1)}, bf16[32,512]{1,0:T(8,128)(2,1)S(1)}, bf16[1024,128]{1,0:T(8,128)(2,1)S(1)}, bf16[2,1024,256]{2,1,0:T(8,128)(2,1)S(1)}, bf16[2,256,1024]{2,1,0:T(8,128)(2,1)S(1)}) custom-call(bf16[32,512]{1,0:T(8,128)(2,1)S(1)} %bitcast.4, bf16[1024,128]{1,0:T(8,128)(2,1)S(1)} %copy-done.2, ...), custom_call_target="tpu_custom_call" | custom-call | tf_op jit(solution)/shard_map/soft_moe/pallas_call | solution.py:455
  123.3 0.6 copy.15
  123.9 0.6 copy.16
  124.6 0.7 copy.17
  125.3 1.0 copy.18
  126.2 1.0 copy.19
Async XLA Ops:
  0.6 1.2 copy-start
  1.9 1.2 copy-start.1
  3.1 0.9 copy-start.2
  4.0 0.8 copy-start.3
  4.8 0.8 copy-start.4

commit v2 on v1

v2 whole, which is shorter than its diff:
```python
import functools
import math

import jax
import jax.numpy as jnp
from jax import lax
from jax.experimental import pallas as pl
from jax.experimental.pallas import tpu as pltpu
from jax.sharding import PartitionSpec as P

MESH = pl.DeviceIdType.MESH
F32 = jnp.float32
BF = jnp.bfloat16
GELU_K = math.sqrt(2.0 / math.pi)

D = 1024
TOK = 256
SLOT = 256
OWN = 128
HID = 256
HALF = 512

(TK_A, TK_B, TK_C, TK_D, CT_A, CT_B, CT_C, CT_D, ROWST, COLST, ROWSUM, COLSUM, MIXX,
 X_SI, R_SI, A_SI, X_DO, R_DO, A_DO, X_GM, R_GM, A_GM, R_SO, A_SO, F_SO, R_DI, A_DI, F_DI,
 MX_A, MX_B, MX_C, GT_A, GT_B, GT_C, NSEM) = range(35)
(L_TOK, L_COT, L_MIX, L_WI, L_WO, L_GWI, L_GWO, L_MX, L_GT, L_GM, NLOC) = range(11)


def dot(a, b):
    return jnp.dot(a, b, preferred_element_type=F32)


def kernel(tok_h, mix_h, win_h, wout_h, cot_h,
           mixed_o, gtok_o, gmix_o, gwin_o, gwout_o,
           tokv, cotv, tt, ct, tn, cn, mh, mt, wi, wo, wit, wot,
           rowst, colst, rowb, colb, rsum, csum, rsumb, csumb,
           pb, xb, sb, rb, ab, pb2, rb2, ab2,
           pz, rz, sz, fz, lt, disp, dispb, combt, combb, dcomb, ddisp, dlog, part1,
           prev, actv, dprev, gwi, gwo, outv, gmv, size,
           ss, rs, ls):
    s = lax.axis_index("seq")
    e = lax.axis_index("expert")
    u, c = s // 2, s % 2
    z, yl = e // 2, e % 2
    r = yl * 8 + u
    p = r * 2 + c

    def dev(u_, yl_, z_, c_):
        return (u_ * 2 + c_, z_ * 2 + yl_)

    def chip(r_, c_):
        return dev(r_ % 8, r_ // 8, z, c_)

    def send(src, dst, k, to, rk=None):
        sent[k] = 1
        pltpu.make_async_remote_copy(
            src_ref=src, dst_ref=dst, send_sem=ss.at[k], recv_sem=rs.at[k if rk is None else rk],
            device_id=to, device_id_type=MESH).start()

    def wait(ref, sem):
        pltpu.make_async_copy(ref, ref, sem).wait()

    sent, got = {}, set()

    def pieces(n):
        return size.at[pl.ds(0, n)]

    REFS = {MIXX: mh.at[0],
            ROWST: rowb.at[pl.ds(0, 15)], COLST: colb.at[pl.ds(0, 31)], ROWSUM: rsumb.at[pl.ds(0, 15)], COLSUM: csumb.at[pl.ds(0, 31)],
            MX_A: pieces(10), MX_B: pieces(8), MX_C: pieces(13), GT_A: pieces(10), GT_B: pieces(8), GT_C: pieces(13)}
    for ka, kb, kc, kd in ((TK_A, TK_B, TK_C, TK_D), (CT_A, CT_B, CT_C, CT_D)):
        REFS.update({ka: pieces(2), kb: pieces(2), kc: pieces(9), kd: pieces(18)})
    for j, kx, kr, ka in ((0, X_SI, R_SI, A_SI), (1, X_DO, R_DO, A_DO), (2, X_GM, R_GM, A_GM)):
        REFS.update({kx: xb.at[j], kr: rb.at[j, pl.ds(0, 15)], ka: rb.at[j, pl.ds(0, 15)]})
    for j, kr, ka, kf in ((0, R_SO, A_SO, F_SO), (1, R_DI, A_DI, F_DI)):
        REFS.update({kr: rb.at[j, pl.ds(0, 15)], ka: rb.at[j, pl.ds(0, 15)], kf: ab2.at[j, 0]})

    def wait_recv(k):
        got.add(k)
        wait(REFS[k], rs.at[k])

    def finish():
        for k in sent:
            if k not in got:
                wait(REFS[k], rs.at[k])
            wait(REFS[k], ss.at[k])

    def local(src, dst, k):
        cp = pltpu.make_async_copy(src, dst, ls.at[k])
        cp.start()
        return cp

    def each(n, f):
        def body(i, carry):
            f(i)
            return carry
        lax.fori_loop(0, n, body, 0)

    for h in range(2):
        local(tok_h.at[:, pl.ds(h * TOK, TOK)], tokv.at[h], L_TOK)
    for h in range(2):
        local(cot_h.at[:, pl.ds(h * TOK, TOK)], cotv.at[h], L_COT)
    local(mix_h, mh.at[yl], L_MIX)
    local(win_h, wi, L_WI)
    local(wout_h, wo, L_WO)

    bar = pltpu.get_barrier_semaphore()

    def sig(to):
        pl.semaphore_signal(bar, inc=1, device_id=to, device_id_type=MESH)

    def sig_plane(i):
        q = (p + 1 + i) % 32
        sig(chip(q // 2, q % 2))
    each(31, sig_plane)
    each(15, lambda i: sig(dev(u, yl, (z + 1 + i) % 16, c)))
    for o in (1, 15, 2, 14, 5, 11):
        sig(dev(u, 1 - yl, (z + o) % 16, c))
    pl.semaphore_wait(bar, 52)

    def zdev(o, yy):
        return dev(u, yy, (z + o) % 16, c)

    def gather1(src, dst, ka, kb, kc):
        for o, k in ((5, ka), (-5, kb), (1, kc), (-1, kc), (2, kc), (-2, kc)):
            for yy in range(2):
                send(src.at[yy], dst.at[z, yl], k, zdev(o + 16, yy))
        send(src.at[1 - yl], dst.at[z, yl], kc, zdev(0, 1 - yl))
        dst[z, yl] = src[yl]

    def gather2(buf, ka, kb, kd):
        wait_recv(ka)
        low = buf.at[(z + 11) % 16]
        for o in (3, 2, -2, 1, -1):
            send(low, low, kd, zdev(o + 16, yl))
        wait_recv(kb)
        high = buf.at[(z + 5) % 16]
        for o in (2, -2, 1, -1):
            send(high, high, kd, zdev(o + 16, yl))

    def gather3(kc, kd):
        wait_recv(kc)
        wait_recv(kd)

    wait(tokv, ls.at[L_TOK])
    gather1(tokv, tt, TK_A, TK_B, TK_C)
    wait(mh.at[0], ls.at[L_MIX])
    send(mh.at[yl], mh.at[yl], MIXX, dev(u, 1 - yl, z, c))
    mt[pl.ds(pl.multiple_of(yl * OWN, OWN), OWN), :] = mh[yl].T
    wait(cotv, ls.at[L_COT])
    gather2(tt, TK_A, TK_B, TK_D)
    gather1(cotv, ct, CT_A, CT_B, CT_C)
    wait_recv(MIXX)
    mt[pl.ds(pl.multiple_of((1 - yl) * OWN, OWN), OWN), :] = mh[1 - yl].T
    wait(wi, ls.at[L_WI])
    wait(wo, ls.at[L_WO])
    for k in range(2):
        wit[k] = wi[k].T
        wot[k] = wo[k].T
    gather3(TK_C, TK_D)

    ttv = tt[...].reshape(D, TOK)
    logits = dot(mt[...], ttv)
    lt[...] = logits
    rm = jnp.max(logits, axis=0, keepdims=True)
    rsm = jnp.sum(jnp.exp(logits - rm), axis=0, keepdims=True)

    def put(ref, at, v):
        ref[at:at + 1, :] = v[:, :128]
        ref[at + 1:at + 2, :] = v[:, 128:]

    put(rowst, 0, rm)
    put(rowst, 2, rsm)

    def z_all(src, dst, k):
        def one(i):
            d = (8 + i // 2 + 1) - 2 * ((i // 2 + 1) * (i % 2))
            send(src, dst.at[z], k, dev(u, yl, (z + d) % 16, c))
        send(src, dst.at[z], k, dev(u, yl, (z + 8) % 16, c))
        each(14, one)
        dst[z] = src[...]

    def plane_all(src, dst, k):
        def one(i):
            q = (p + 1 + i) % 32
            send(src, dst.at[p], k, chip(q // 2, q % 2))
        each(31, one)
        dst[p] = src[...]

    def to_row(col):
        return jnp.broadcast_to(col, (SLOT, 128)).T[0:1, :]

    def to_cols(two):
        row = jnp.concatenate([two[0:1, :], two[1:2, :]], axis=1)
        half = jnp.broadcast_to(row, (128, SLOT)).T
        return jnp.concatenate([half, half], axis=1)

    z_all(rowst, rowb, ROWST)
    gather2(ct, CT_A, CT_B, CT_D)
    cm = jnp.max(logits, axis=1, keepdims=True)
    csm = jnp.sum(jnp.exp(logits - cm), axis=1, keepdims=True)
    put(colst, 0, to_row(cm))
    put(colst, 2, to_row(csm))
    plane_all(colst, colb, COLST)

    tn[...] = ttv.T

    def totals(buf):
        v = buf[...]
        m = v[:, 0:2, :]
        top = jnp.max(m, axis=0)
        total = jnp.sum(v[:, 2:4, :] * jnp.exp(m - top[None]), axis=0)
        return top, total

    def core_swap(buf, xbuf, k):
        send(buf.at[1 - c], xbuf, k, dev(u, yl, z, 1 - c))

    def store_halves(buf, v):
        n = v.shape[0]
        for h in range(2):
            buf[h] = v[:, h * HALF:(h + 1) * HALF].astype(BF).reshape(n // 16, 16, HALF)

    def rs32_send(j, kx, kr):
        wait_recv(kx)
        sb[j] = (pb[j, c].astype(F32) + xb[j].astype(F32)).astype(BF)

        def one(i):
            q = (r + 1 + i) % 16
            send(sb.at[j, q], rb.at[j, r], kr, chip(q, c))
        each(15, one)
        rb[j, r] = sb[j, r]

    def rs32_sum(j, kr):
        wait_recv(kr)
        return jnp.sum(rb[j].astype(F32), axis=0).astype(BF)

    me = u * 2 + c

    def mate(i):
        q = (me + 1 + i) % 16
        return q // 2, q % 2

    def ag16_send(j, v, ka):
        ab[j, c, u] = v

        def one(i):
            qu, qc = mate(i)
            send(ab.at[j, c, u], ab.at[j, c, u], ka, dev(qu, yl, z, qc))
        each(15, one)

    wait_recv(COLST)
    top, total = totals(colb)
    dv = jnp.exp(lt[...] - to_cols(top)) / to_cols(total)
    disp[...] = dv
    dispb[...] = dv.astype(BF)
    store_halves(pb.at[0], dot(dispb[...], tn[...]))
    core_swap(pb.at[0], xb.at[0], X_SI)
    gather3(CT_C, CT_D)
    cn[...] = ct[...].reshape(D, TOK).T
    rs32_send(0, X_SI, R_SI)

    wait_recv(ROWST)
    top, total = totals(rowb)
    topr = jnp.concatenate([top[0:1, :], top[1:2, :]], axis=1)
    totr = jnp.concatenate([total[0:1, :], total[1:2, :]], axis=1)
    cv = jnp.exp(lt[...] - topr) / totr
    combt[...] = cv
    combb[...] = cv.astype(BF)
    store_halves(pb.at[1], dot(combb[...], cn[...]))
    core_swap(pb.at[1], xb.at[1], X_DO)
    rs32_send(1, X_DO, R_DO)
    ag16_send(0, rs32_sum(0, R_SI), A_SI)
    ag16_send(1, rs32_sum(1, R_DO), A_DO)

    def halves(j):
        return [ab[j, h].reshape(OWN, HALF) for h in range(2)]

    def rs16_send(j, v, kr):
        store_halves(pb2.at[j], v)

        def one(i):
            qu, qc = mate(i)
            send(pb2.at[j, qc, qu], rb2.at[j, me], kr, dev(qu, yl, z, qc))
        each(15, one)
        rb2[j, me] = pb2[j, c, u]

    def rs16_sum(j, kr):
        wait_recv(kr)
        return jnp.sum(rb2[j].astype(F32), axis=0).astype(BF)

    def ag32_send(j, v, ka):
        ab2[j, c, r] = v

        def one(i):
            q = (r + 1 + i) % 16
            send(ab2.at[j, c, r], ab2.at[j, c, r], ka, chip(q, c))
        each(15, one)

    def ag32_forward(j, ka, kf):
        wait_recv(ka)
        send(ab2.at[j, c], ab2.at[j, c], kf, dev(u, yl, z, 1 - c))

    def rows(k):
        return slice(k * 64, (k + 1) * 64)

    wait_recv(A_SI)
    x0, x1 = halves(0)
    outs = []
    for k in range(2):
        pre = dot(x0[rows(k)], wi[k, :HALF, :]) + dot(x1[rows(k)], wi[k, HALF:, :])
        prev[k] = pre
        t = jnp.tanh(GELU_K * (pre + 0.044715 * (pre * pre * pre)))
        act = (0.5 * pre * (1.0 + t)).astype(BF)
        actv[k] = act
        outs.append(dot(act, wo[k]))
    rs16_send(0, jnp.concatenate(outs, axis=0), R_SO)

    wait_recv(A_DO)
    g0, g1 = halves(1)
    outs = []
    for k in range(2):
        dact = dot(g0[rows(k)], wot[k, :HALF, :]) + dot(g1[rows(k)], wot[k, HALF:, :])
        pre = prev[k]
        sq = pre * pre
        t = jnp.tanh(GELU_K * (pre + 0.044715 * (sq * pre)))
        slope = 0.5 * (1.0 + t) + 0.5 * pre * (1.0 - t * t) * (GELU_K * (1.0 + 3.0 * 0.044715 * sq))
        dpre = (dact * slope).astype(BF)
        dprev[k] = dpre
        outs.append(dot(dpre, wit[k]))
    rs16_send(1, jnp.concatenate(outs, axis=0), R_DI)
    ag32_send(0, rs16_sum(0, R_SO), A_SO)

    for k in range(2):
        xt0, xt1 = x0[rows(k)].T, x1[rows(k)].T
        gwi[k, :HALF, :] = dot(xt0, dprev[k]).astype(BF)
        gwi[k, HALF:, :] = dot(xt1, dprev[k]).astype(BF)
        at = actv[k].T
        gwo[k, :, :HALF] = dot(at, g0[rows(k)]).astype(BF)
        gwo[k, :, HALF:] = dot(at, g1[rows(k)]).astype(BF)
    local(gwi, gwin_o, L_GWI)
    local(gwo, gwout_o, L_GWO)

    ag32_send(1, rs16_sum(1, R_DI), A_DI)
    ag32_forward(0, A_SO, F_SO)

    def full(j):
        return [ab2[j, h].reshape(SLOT, HALF) for h in range(2)]

    def scatter1(j, ka, kb, kc):
        src = pz.at[j]

        def at(o):
            return (z + o + 16) % 16
        for i, o in enumerate((2, -2, 1, -1)):
            if i == 0:
                send(src.at[at(8)], rz.at[j, 0, 4], ka, zdev(3, yl))
            send(src.at[at(o + 5)], rz.at[j, 0, i], ka, zdev(o + 16, yl))
            send(src.at[at(o - 5)], rz.at[j, 1, i], kb, zdev(o + 16, yl))
        for i, o in enumerate((2, -2, 1, -1)):
            for yy in range(2):
                send(src.at[at(o), yy], fz.at[j, 1 + i, yl], kc, zdev(o + 16, yy))
        send(src.at[z, 1 - yl], fz.at[j, 0, yl], kc, zdev(0, 1 - yl))

    def scatter2(j, ka, kb, kc):
        for h, k, o, n in ((0, ka, 5, 5), (1, kb, -5, 4)):
            wait_recv(k)
            v = pz[j, (z + o + 16) % 16].astype(F32)
            for i in range(n):
                v = v + rz[j, h, i].astype(F32)
            sz[j, h] = v.astype(BF)
            for yy in range(2):
                send(sz.at[j, h, yy], fz.at[j, 5 + h, yl], kc, zdev(o + 16, yy))
        fz[j, 0, yl] = pz[j, z, yl]

    def scatter3(j, k2, out, lk):
        wait_recv(k2)
        v = jnp.sum(fz[j].astype(F32), axis=0).astype(BF)
        for h in range(2):
            outv[j, :, h * TOK:(h + 1) * TOK] = v[h]
        local(outv.at[j], out, lk)

    wait_recv(F_SO)
    so0, so1 = full(0)
    ctv = ct[...].reshape(D, TOK)
    dcv = dot(so0, ctv[:HALF]) + dot(so1, ctv[HALF:])
    dcomb[...] = dcv
    put(rsum, 0, jnp.sum(combt[...] * dcv, axis=0, keepdims=True))
    z_all(rsum, rsumb, ROWSUM)
    ag32_forward(1, A_DI, F_DI)
    pz[0, 0:8] = dot(so0.T, combb[...]).astype(BF).reshape(8, 2, 32, TOK)
    pz[0, 8:16] = dot(so1.T, combb[...]).astype(BF).reshape(8, 2, 32, TOK)
    scatter1(0, MX_A, MX_B, MX_C)

    wait_recv(F_DI)
    di0, di1 = full(1)
    ddv = dot(di0, ttv[:HALF]) + dot(di1, ttv[HALF:])
    ddisp[...] = ddv
    put(csum, 0, to_row(jnp.sum(disp[...] * ddv, axis=1, keepdims=True)))
    plane_all(csum, csumb, COLSUM)

    part1[0:HALF, :] = dot(di0.T, dispb[...])
    part1[HALF:, :] = dot(di1.T, dispb[...])
    wait_recv(COLSUM)
    cols = to_cols(jnp.sum(csumb[...], axis=0))
    wait_recv(ROWSUM)
    rtot = jnp.sum(rsumb[...], axis=0)
    rowr = jnp.concatenate([rtot[0:1, :], rtot[1:2, :]], axis=1)
    dlv = (disp[...] * (ddisp[...] - cols) + combt[...] * (dcomb[...] - rowr)).astype(BF)
    dlog[...] = dlv
    store_halves(pb.at[2], dot(dlog[...], tn[...]))
    core_swap(pb.at[2], xb.at[2], X_GM)
    mfull = jnp.concatenate([mh[0], mh[1]], axis=1)
    pz[1] = (part1[...] + dot(mfull, dlv)).astype(BF).reshape(16, 2, 32, TOK)
    scatter1(1, GT_A, GT_B, GT_C)
    rs32_send(2, X_GM, R_GM)
    scatter2(0, MX_A, MX_B, MX_C)
    scatter2(1, GT_A, GT_B, GT_C)
    ag16_send(2, rs32_sum(2, R_GM), A_GM)
    scatter3(0, MX_C, mixed_o, L_MX)
    scatter3(1, GT_C, gtok_o, L_GT)
    wait_recv(A_GM)
    for h in range(2):
        gmv[h * HALF:(h + 1) * HALF, :] = ab[2, h].reshape(OWN, HALF).T
    local(gmv, gmix_o, L_GM)

    finish()
    wait(gwi, ls.at[L_GWI])
    wait(gwo, ls.at[L_GWO])
    wait(outv.at[0], ls.at[L_MX])
    wait(outv.at[1], ls.at[L_GT])
    wait(gmv, ls.at[L_GM])


def write_out(*refs):
    n = 5
    src, dst, held = refs[:n], refs[n:2 * n], refs[2 * n:3 * n]
    sem = refs[3 * n]
    loads = [pltpu.make_async_copy(src[i], held[i], sem.at[0, i]) for i in range(n)]
    stores = [pltpu.make_async_copy(held[i], dst[i], sem.at[1, i]) for i in range(n)]
    for cp in loads:
        cp.start()
    for i in range(n):
        loads[i].wait()
        stores[i].start()
    for cp in stores:
        cp.wait()


def per_device(tokens, mix, w_in, w_out, cotangent):
    scratch = [
        ((2, 32, TOK), BF), ((2, 32, TOK), BF),
        ((16, 2, 32, TOK), BF), ((16, 2, 32, TOK), BF),
        ((TOK, D), BF), ((TOK, D), BF),
        ((2, D, OWN), BF), ((SLOT, D), BF),
        ((2, D, HID), BF), ((2, HID, D), BF),
        ((2, HID, D), BF), ((2, D, HID), BF),
        ((8, 128), F32), ((8, 128), F32), ((16, 8, 128), F32), ((32, 8, 128), F32),
        ((8, 128), F32), ((8, 128), F32), ((16, 8, 128), F32), ((32, 8, 128), F32),
        ((3, 2, 16, 16, HALF), BF), ((3, 16, 16, HALF), BF), ((3, 16, 16, HALF), BF),
        ((3, 16, 16, HALF), BF), ((3, 2, 8, 16, HALF), BF),
        ((2, 2, 8, 16, HALF), BF), ((2, 16, 16, HALF), BF), ((2, 2, 16, 16, HALF), BF),
        ((2, 16, 2, 32, TOK), BF), ((2, 2, 5, 2, 32, TOK), BF),
        ((2, 2, 2, 32, TOK), BF), ((2, 7, 2, 32, TOK), BF),
        ((SLOT, TOK), F32), ((SLOT, TOK), F32), ((SLOT, TOK), BF), ((SLOT, TOK), F32), ((SLOT, TOK), BF),
        ((SLOT, TOK), F32), ((SLOT, TOK), F32), ((SLOT, TOK), BF), ((D, TOK), F32),
        ((2, 64, HID), F32), ((2, 64, HID), BF), ((2, 64, HID), BF),
        ((2, D, HID), BF), ((2, HID, D), BF), ((2, 32, 2 * TOK), BF), ((D, OWN), BF),
        ((18, 32, TOK), BF),
    ]
    hbm = pl.BlockSpec(memory_space=pl.ANY)
    results = pl.pallas_call(
        kernel,
        out_shape=(
            jax.ShapeDtypeStruct((32, 512), BF),
            jax.ShapeDtypeStruct((32, 512), BF),
            jax.ShapeDtypeStruct(mix.shape, BF),
            jax.ShapeDtypeStruct(w_in.shape, BF),
            jax.ShapeDtypeStruct(w_out.shape, BF),
        ),
        in_specs=[hbm] * 5,
        out_specs=[hbm] * 5,
        scratch_shapes=[pltpu.VMEM(shape, kind) for shape, kind in scratch] + [
            pltpu.SemaphoreType.DMA((NSEM,)),
            pltpu.SemaphoreType.DMA((NSEM,)),
            pltpu.SemaphoreType.DMA((NLOC,)),
        ],
        compiler_params=pltpu.CompilerParams(
            collective_id=0, has_side_effects=True, vmem_limit_bytes=63 * 1024 * 1024
        ),
        name="soft_moe",
    )(tokens.T, mix, w_in, w_out, cotangent.T)
    mixed_t, gtok_t, gmix, gwin, gwout = pl.pallas_call(
        write_out,
        out_shape=tuple(jax.ShapeDtypeStruct(v.shape, v.dtype) for v in results),
        in_specs=[hbm] * 5,
        out_specs=tuple([hbm] * 5),
        scratch_shapes=[pltpu.VMEM(v.shape, v.dtype) for v in results] + [pltpu.SemaphoreType.DMA((2, 5))],
        compiler_params=pltpu.CompilerParams(vmem_limit_bytes=63 * 1024 * 1024),
        name="write_out",
    )(*results)
    return mixed_t.T, gtok_t.T, gmix, gwin, gwout


def solution(mesh):
    placed = (
        P("seq", "expert"),
        P(None, "expert"),
        P("expert", None, "seq"),
        P("expert", "seq", None),
        P("seq", "expert"),
    )
    return jax.shard_map(
        per_device,
        mesh=mesh,
        in_specs=placed,
        out_specs=(
            P("seq", "expert"),
            P("seq", "expert"),
            P(None, "expert"),
            P("expert", None, "seq"),
            P("expert", "seq", None),
        ),
        check_vma=False,
    )
```

time: 128 us -> 108 us (0.84)
  Pallas kernels: 118 us -> 107 us
  local copies, waits for them, and re-layouts: 8.78 us -> 0 us
    pallas_call x1, Pallas kernels: 118 us -> 104 us  [per_device(): pl.pallas_call(kernel, out_shape=(jax.ShapeDtypeStruct((32, 512), BF), ja...]
    unnamed x15 -> x0, local copies, waits for them, and re-layouts: 8.78 us -> none
    pallas_call x0 -> x1, Pallas kernels: none -> 2.75 us  [per_device(): pl.pallas_call(write_out, out_shape=tuple((jax.ShapeDtypeStruct(v.shape,...]
where the time goes in v2:
time: 108 us; the launch traced here: 107 us
  Pallas kernels  107 us (99%)
    pallas_call x1, Pallas kernels, per_device(): pl.pallas_call(kernel, out_shape=(jax.ShapeDtypeStruct((32, 512), BF), ja...  104 us
    pallas_call x1, Pallas kernels, per_device(): pl.pallas_call(write_out, out_shape=tuple((jax.ShapeDtypeStruct(v.shape,...  2.75 us

profile of v2, /device:TPU:1, one launch (start us, length us, event | category | flops | bytes accessed | tf_op | source)
XLA Modules:
  0.0 107.4 jit_solution(8338519501535962104)
XLA Ops:
  0.6 104.0 %soft_moe.1 = (bf16[32,512]{1,0:T(8,128)(2,1)}, bf16[32,512]{1,0:T(8,128)(2,1)}, bf16[1024,128]{1,0:T(8,128)(2,1)}, bf16[2,1024,256]{2,1,0:T(8,128)(2,1)}, bf16[2,256,1024]{2,1,0:T(8,128)(2,1)}) custom-call(bf16[32,512]{1,0:T(8,128)(2,1)} %bitcast.4, bf16[1024,128]{1,0:T(8,128)(2,1)} %mix_h.1, bf16[2,1024,256]{2,1,0:T(8,128)(2,1)} %win_h.1, ...), custom_call_target="tpu_custom_call" | custom-call | tf_op jit(solution)/shard_map/soft_moe/pallas_call | solution.py:471
  104.6 2.7 %write_out.1 = (bf16[32,512]{1,0:T(8,128)(2,1)}, bf16[32,512]{1,0:T(8,128)(2,1)}, bf16[1024,128]{1,0:T(8,128)(2,1)}, bf16[2,1024,256]{2,1,0:T(8,128)(2,1)}, bf16[2,256,1024]{2,1,0:T(8,128)(2,1)}) custom-call(bf16[32,512]{1,0:T(8,128)(2,1)} %get-tuple-element.15.refs_0_, bf16[32,512]{1,0:T(8,128)(2,1)} %get-tuple-element.16.refs_1_, ...), custom_call_target="tpu_custom_call" | custom-call | tf_op jit(solution)/shard_map/write_out/pallas_call | solution.py:492

commit v3 on v2

--- a/solution.py
+++ b/solution.py
@@ -43,13 +43,22 @@
     u, c = s // 2, s % 2
     z, yl = e // 2, e % 2
     r = yl * 8 + u
-    p = r * 2 + c
+    p = s * 2 + yl
+    flip_s = [2 ** k * (1 - 2 * ((s // 2 ** k) % 2)) for k in range(4)]
+    flip_e = [2 ** k * (1 - 2 * ((e // 2 ** k) % 2)) for k in range(5)]
+    flip_u = [2 ** k * (1 - 2 * ((u // 2 ** k) % 2)) for k in range(3)] + [8 * (1 - 2 * yl)]
+
+    def flipped(v, weights, j):
+        for k, w in enumerate(weights):
+            if (j >> k) % 2:
+                v = v + w
+        return v
+
+    def peer(j, b=0):
+        return flipped(s, flip_s, j), flipped(e, flip_e, b)
 
     def dev(u_, yl_, z_, c_):
         return (u_ * 2 + c_, z_ * 2 + yl_)
-
-    def chip(r_, c_):
-        return dev(r_ % 8, r_ // 8, z, c_)
 
     def send(src, dst, k, to, rk=None):
         sent[k] = 1
@@ -90,12 +99,6 @@
         cp.start()
         return cp
 
-    def each(n, f):
-        def body(i, carry):
-            f(i)
-            return carry
-        lax.fori_loop(0, n, body, 0)
-
     for h in range(2):
         local(tok_h.at[:, pl.ds(h * TOK, TOK)], tokv.at[h], L_TOK)
     for h in range(2):
@@ -109,13 +112,12 @@
     def sig(to):
         pl.semaphore_signal(bar, inc=1, device_id=to, device_id_type=MESH)
 
-    def sig_plane(i):
-        q = (p + 1 + i) % 32
-        sig(chip(q // 2, q % 2))
-    each(31, sig_plane)
-    each(15, lambda i: sig(dev(u, yl, (z + 1 + i) % 16, c)))
+    for d in (8, 9, 7, 10, 6, 11, 5, 12, 4, 13, 3, 14, 2, 15, 1):
+        sig(dev(u, yl, (z + d) % 16, c))
     for o in (1, 15, 2, 14, 5, 11):
         sig(dev(u, 1 - yl, (z + o) % 16, c))
+    for i in range(31, 0, -1):
+        sig(peer(i // 2, i % 2))
     pl.semaphore_wait(bar, 52)
 
     def zdev(o, yy):
@@ -173,18 +175,13 @@
     put(rowst, 2, rsm)
 
     def z_all(src, dst, k):
-        def one(i):
-            d = (8 + i // 2 + 1) - 2 * ((i // 2 + 1) * (i % 2))
-            send(src, dst.at[z], k, dev(u, yl, (z + d) % 16, c))
-        send(src, dst.at[z], k, dev(u, yl, (z + 8) % 16, c))
-        each(14, one)
+        for d in (8, 9, 7, 10, 6, 11, 5, 12, 4, 13, 3, 14, 2, 15, 1):
+            send(src, dst.at[z], k, zdev(d, yl))
         dst[z] = src[...]
 
     def plane_all(src, dst, k):
-        def one(i):
-            q = (p + 1 + i) % 32
-            send(src, dst.at[p], k, chip(q // 2, q % 2))
-        each(31, one)
+        for i in range(31, 0, -1):
+            send(src, dst.at[p], k, peer(i // 2, i % 2))
         dst[p] = src[...]
 
     def to_row(col):
@@ -196,12 +193,12 @@
         return jnp.concatenate([half, half], axis=1)
 
     z_all(rowst, rowb, ROWST)
-    gather2(ct, CT_A, CT_B, CT_D)
     cm = jnp.max(logits, axis=1, keepdims=True)
     csm = jnp.sum(jnp.exp(logits - cm), axis=1, keepdims=True)
     put(colst, 0, to_row(cm))
     put(colst, 2, to_row(csm))
     plane_all(colst, colb, COLST)
+    gather2(ct, CT_A, CT_B, CT_D)
 
     tn[...] = ttv.T
 
@@ -224,29 +221,18 @@
         wait_recv(kx)
         sb[j] = (pb[j, c].astype(F32) + xb[j].astype(F32)).astype(BF)
 
-        def one(i):
-            q = (r + 1 + i) % 16
-            send(sb.at[j, q], rb.at[j, r], kr, chip(q, c))
-        each(15, one)
+        for i in range(15, 0, -1):
+            send(sb.at[j, flipped(r, flip_u, i)], rb.at[j, r], kr, peer(2 * (i % 8), i // 8))
         rb[j, r] = sb[j, r]
 
     def rs32_sum(j, kr):
         wait_recv(kr)
         return jnp.sum(rb[j].astype(F32), axis=0).astype(BF)
 
-    me = u * 2 + c
-
-    def mate(i):
-        q = (me + 1 + i) % 16
-        return q // 2, q % 2
-
     def ag16_send(j, v, ka):
         ab[j, c, u] = v
-
-        def one(i):
-            qu, qc = mate(i)
-            send(ab.at[j, c, u], ab.at[j, c, u], ka, dev(qu, yl, z, qc))
-        each(15, one)
+        for i in range(15, 0, -1):
+            send(ab.at[j, c, u], ab.at[j, c, u], ka, peer(i))
 
     wait_recv(COLST)
     top, total = totals(colb)
@@ -277,12 +263,10 @@
 
     def rs16_send(j, v, kr):
         store_halves(pb2.at[j], v)
-
-        def one(i):
-            qu, qc = mate(i)
-            send(pb2.at[j, qc, qu], rb2.at[j, me], kr, dev(qu, yl, z, qc))
-        each(15, one)
-        rb2[j, me] = pb2[j, c, u]
+        for i in range(15, 0, -1):
+            qu, qc = flipped(u, flip_u, i // 2), flipped(c, flip_s[:1], i % 2)
+            send(pb2.at[j, qc, qu], rb2.at[j, s], kr, peer(i))
+        rb2[j, s] = pb2[j, c, u]
 
     def rs16_sum(j, kr):
         wait_recv(kr)
@@ -290,11 +274,8 @@
 
     def ag32_send(j, v, ka):
         ab2[j, c, r] = v
-
-        def one(i):
-            q = (r + 1 + i) % 16
-            send(ab2.at[j, c, r], ab2.at[j, c, r], ka, chip(q, c))
-        each(15, one)
+        for i in range(15, 0, -1):
+            send(ab2.at[j, c, r], ab2.at[j, c, r], ka, peer(2 * (i % 8), i // 8))
 
     def ag32_forward(j, ka, kf):
         wait_recv(ka)
@@ -379,10 +360,15 @@
             outv[j, :, h * TOK:(h + 1) * TOK] = v[h]
         local(outv.at[j], out, lk)
 
-    wait_recv(F_SO)
+    def by_halves(j, kf, buf):
+        def part(h):
+            return dot(ab2[j, h].reshape(SLOT, HALF), buf[pl.ds(h * 8, 8)].reshape(HALF, TOK))
+        v = part(c)
+        wait_recv(kf)
+        return v + part(1 - c)
+
+    dcv = by_halves(0, F_SO, ct)
     so0, so1 = full(0)
-    ctv = ct[...].reshape(D, TOK)
-    dcv = dot(so0, ctv[:HALF]) + dot(so1, ctv[HALF:])
     dcomb[...] = dcv
     put(rsum, 0, jnp.sum(combt[...] * dcv, axis=0, keepdims=True))
     z_all(rsum, rsumb, ROWSUM)
@@ -391,9 +377,8 @@
     pz[0, 8:16] = dot(so1.T, combb[...]).astype(BF).reshape(8, 2, 32, TOK)
     scatter1(0, MX_A, MX_B, MX_C)
 
-    wait_recv(F_DI)
+    ddv = by_halves(1, F_DI, tt)
     di0, di1 = full(1)
-    ddv = dot(di0, ttv[:HALF]) + dot(di1, ttv[HALF:])
     ddisp[...] = ddv
     put(csum, 0, to_row(jnp.sum(disp[...] * ddv, axis=1, keepdims=True)))
     plane_all(csum, csumb, COLSUM)

time: 108 us -> 108 us (level)
  no operation moved by 1% of the time
where the time goes in v3:
time: 108 us
  Pallas kernels  108 us (100%)
    pallas_call x1, Pallas kernels, per_device(): pl.pallas_call(kernel, out_shape=(jax.ShapeDtypeStruct((32, 512), BF), ja...  105 us
    pallas_call x1, Pallas kernels, per_device(): pl.pallas_call(write_out, out_shape=tuple((jax.ShapeDtypeStruct(v.shape,...  2.75 us

profile of v3, /device:TPU:1, one launch (start us, length us, event | category | flops | bytes accessed | tf_op | source)
XLA Modules:
  0.0 108.2 jit_solution(4626221174778013645)
XLA Ops:
  0.6 104.8 %soft_moe.1 = (bf16[32,512]{1,0:T(8,128)(2,1)}, bf16[32,512]{1,0:T(8,128)(2,1)}, bf16[1024,128]{1,0:T(8,128)(2,1)}, bf16[2,1024,256]{2,1,0:T(8,128)(2,1)}, bf16[2,256,1024]{2,1,0:T(8,128)(2,1)}) custom-call(bf16[32,512]{1,0:T(8,128)(2,1)} %bitcast.4, bf16[1024,128]{1,0:T(8,128)(2,1)} %mix_h.1, bf16[2,1024,256]{2,1,0:T(8,128)(2,1)} %win_h.1, ...), custom_call_target="tpu_custom_call" | custom-call | tf_op jit(solution)/shard_map/soft_moe/pallas_call | solution.py:456
  105.4 2.7 %write_out.1 = (bf16[32,512]{1,0:T(8,128)(2,1)}, bf16[32,512]{1,0:T(8,128)(2,1)}, bf16[1024,128]{1,0:T(8,128)(2,1)}, bf16[2,1024,256]{2,1,0:T(8,128)(2,1)}, bf16[2,256,1024]{2,1,0:T(8,128)(2,1)}) custom-call(bf16[32,512]{1,0:T(8,128)(2,1)} %get-tuple-element.15.refs_0_, bf16[32,512]{1,0:T(8,128)(2,1)} %get-tuple-element.16.refs_1_, ...), custom_call_target="tpu_custom_call" | custom-call | tf_op jit(solution)/shard_map/write_out/pallas_call | solution.py:477
